TPU v7x, 512 devices: a whole 4x4x16 slice. The times are simulated.
512 devices in a mesh: coef: 8 (over y, x_lo), grid: 64 (over z, x_hi, core).
Axes of the slice: x: 4 (x_hi: 2, x_lo: 2; x = x_hi * 2 + x_lo), y: 4, z: 16, core: 2. Of those that a mesh axis runs over, the one named last changes fastest.
Arguments:
- basis_values: bfloat16 [40960, 2688], P('grid'), may hold values from -6 to 6
- occ_coef: bfloat16 [40960, 1024], P('grid', 'coef'), may hold values from -0.125 to 0.125
- listed_panels: int32 [64, 21], P('grid'), may hold values from 0 to 319, as said below
- centres: float32 [3, 40960], replicated, may hold values from 0 to 4
- point_weights: float32 [40960], P('grid'), may hold values from 0.25 to 4
Outputs:
- exchange_tiles: float32 [40960, 1024], P('grid', 'coef')
Inputs may be any that keep to these rules, and one draw needn't show every extreme that they name: `listed_panels`: the panels of one batch are distinct; panel p belongs to batch p // 5, and batch b names only panels of batches b - 4 to b + 4.
All inputs are finite; a program needn't handle non-finite values.
Results may differ from a plain program's by a relative error of at most 0.0085.
Values may be sent and summed in bfloat16 or wider, within the bound.
A program may use at most 64 MiB of HBM per device.

v0:
```python
import jax
import jax.numpy as jnp
from jax import lax
from jax.sharding import PartitionSpec as P

ORBITALS = 1024
PANEL_ROWS = 128
PANELS_DEV = 5
REACH = 4
LISTED = 21


def from_behind(block, axis, distance):
    devices = range(lax.axis_size(axis))
    route = [(i - distance, i) for i in devices if i - distance in devices]
    return lax.ppermute(block, axis, route)


def padded(block, sides, width):
    for axis, dim in sides:
        count = lax.axis_size(axis)
        forward = [(i, i + 1) for i in range(count - 1)]
        backward = [(target, source) for source, target in forward]
        low = lax.ppermute(
            lax.slice_in_dim(block, block.shape[dim] - width, None, axis=dim), axis, forward
        )
        high = lax.ppermute(lax.slice_in_dim(block, 0, width, axis=dim), axis, backward)
        block = jnp.concatenate([low, block, high], axis=dim)
    return block


def nearby(panels, offset):
    return from_behind(panels, "grid", -offset)


def send_back(contrib, offset):
    return from_behind(contrib.astype(jnp.bfloat16), "grid", offset).astype(contrib.dtype)


def shards(basis_values, occ_coef, listed_panels, centres, point_weights):
    width = occ_coef.shape[1]
    points = basis_values.shape[0]
    panels = occ_coef.reshape(PANELS_DEV, PANEL_ROWS, width)
    listed = listed_panels[0]
    batch = lax.axis_index("grid")
    pieces = {0: panels}
    for offset in range(-REACH, REACH + 1):
        if offset != 0:
            pieces[offset] = nearby(panels, offset)
    candidates = jnp.concatenate([pieces[offset] for offset in range(-REACH, REACH + 1)], 0)
    chosen = jnp.take(candidates, listed - (batch - REACH) * PANELS_DEV, axis=0)
    field = jnp.dot(
        basis_values, chosen.reshape(LISTED * PANEL_ROWS, width), preferred_element_type=jnp.float32
    ).astype(jnp.bfloat16)
    near = padded(field, (("grid", 0),), points)
    partial_value = lax.dot_general(
        field, near, (((1,), (1,)), ((), ())), preferred_element_type=jnp.float32
    )
    partial_value = partial_value / jnp.sqrt(jnp.float32(ORBITALS))
    density = lax.psum(partial_value.astype(jnp.bfloat16), "coef").astype(jnp.float32)
    anchor = jnp.zeros((), jnp.int32)
    start = batch * points
    padded_centres = jnp.pad(centres, ((0, 0), (points, points)))
    own_centres = lax.dynamic_slice(centres, (anchor, start), (3, points))
    near_centres = lax.dynamic_slice(padded_centres, (anchor, start), (3, 3 * points))
    distance = jnp.zeros((points, 3 * points), jnp.float32)
    for axis in range(3):
        gap = own_centres[axis][:, None] - near_centres[axis][None, :]
        distance = distance + gap * gap
    kernel = 1.0 / jnp.sqrt(distance + 0.25)
    mixed = (kernel * density).astype(jnp.bfloat16)
    exchanged = jnp.dot(mixed, near, preferred_element_type=jnp.float32)
    weighted = (exchanged * point_weights[:, None] / jnp.sqrt(jnp.float32(3 * points))).astype(
        jnp.bfloat16
    )
    tiles = lax.dot_general(
        basis_values, weighted, (((0,), (0,)), ((), ())), preferred_element_type=jnp.float32
    )
    tiles = (tiles / jnp.sqrt(jnp.float32(points))).reshape(LISTED, PANEL_ROWS, width)
    contribs = {}
    for offset in range(-REACH, REACH + 1):
        first_panel = (batch + offset) * PANELS_DEV
        select = (
            listed[None, :] == first_panel + jnp.arange(PANELS_DEV, dtype=jnp.int32)[:, None]
        ).astype(jnp.float32)
        contribs[offset] = jnp.einsum("js,sro->jro", select, tiles)
    total = contribs[0]
    for offset in range(-REACH, REACH + 1):
        if offset != 0:
            total = total + send_back(contribs[offset], offset)
    return total.reshape(PANELS_DEV * PANEL_ROWS, width)


def solution(mesh):
    placed = (P("grid", None), P("grid", "coef"), P("grid", None), P(), P("grid"))
    return jax.shard_map(
        shards, mesh=mesh, in_specs=placed, out_specs=P("grid", "coef"), check_vma=False
    )
```

profile of v0, /device:TPU:388, one launch (start us, length us, event | category | flops | bytes accessed | tf_op | source)
XLA Modules:
  0.0 277.5 jit_solution(35657123346483395)
XLA Ops:
  6.5 3.2 %collective-permute-start = (bf16[5,128,128]{2,1,0:T(8,128)(2,1)}, bf16[5,128,128]{2,1,0:T(8,128)(2,1)}, u32[]{:S(2)}, u32[]{:S(2)}) collective-permute-start(bf16[5,128,128]{2,1,0:T(8,128)(2,1)} %bitcast.62), channel_id=1, source_target_pairs={{0,4},{1,5},{2,6},{3,7},{4,8},{5,9},{6,10},{7,11},{8,12},{9,13},{1... | collective-permute-start | bytes 491528 | tf_op jit(solution)/shard_map/ppermute | solution.py:16
  11.8 4.9 %collective-permute-start.2 = (bf16[5,128,128]{2,1,0:T(8,128)(2,1)}, bf16[5,128,128]{2,1,0:T(8,128)(2,1)}, u32[]{:S(2)}, u32[]{:S(2)}) collective-permute-start(bf16[5,128,128]{2,1,0:T(8,128)(2,1)} %bitcast.64), channel_id=1, source_target_pairs={{0,2},{1,3},{2,4},{3,5},{4,6},{5,7},{6,8},{7,9},{8,10},{9,11},{10,... | collective-permute-start | bytes 491528 | tf_op jit(solution)/shard_map/ppermute | solution.py:16
  18.6 5.1 %collective-permute-start.4 = (bf16[5,128,128]{2,1,0:T(8,128)(2,1)}, bf16[5,128,128]{2,1,0:T(8,128)(2,1)}, u32[]{:S(2)}, u32[]{:S(2)}) collective-permute-start(bf16[5,128,128]{2,1,0:T(8,128)(2,1)} %bitcast.66), channel_id=1, source_target_pairs={{1,0},{2,1},{3,2},{4,3},{5,4},{6,5},{7,6},{8,7},{9,8},{10,9},{11,1... | collective-permute-start | bytes 491528 | tf_op jit(solution)/shard_map/ppermute | solution.py:16
  25.2 4.5 %collective-permute-start.5 = (bf16[5,128,128]{2,1,0:T(8,128)(2,1)}, bf16[5,128,128]{2,1,0:T(8,128)(2,1)S(1)}, u32[]{:S(2)}, u32[]{:S(2)}) collective-permute-start(bf16[5,128,128]{2,1,0:T(8,128)(2,1)} %bitcast.67), channel_id=1, source_target_pairs={{2,0},{3,1},{4,2},{5,3},{6,4},{7,5},{8,6},{9,7},{10,8},{11,9},{12,... | collective-permute-start | bytes 491528 | tf_op jit(solution)/shard_map/ppermute | solution.py:16
  34.8 2.9 %collective-permute-start.7 = (bf16[5,128,128]{2,1,0:T(8,128)(2,1)}, bf16[5,128,128]{2,1,0:T(8,128)(2,1)S(1)}, u32[]{:S(2)}, u32[]{:S(2)}) collective-permute-start(bf16[5,128,128]{2,1,0:T(8,128)(2,1)} %bitcast.69), channel_id=1, source_target_pairs={{4,0},{5,1},{6,2},{7,3},{8,4},{9,5},{10,6},{11,7},{12,8},{13,9},{1... | collective-permute-start | bytes 491528 | tf_op jit(solution)/shard_map/ppermute | solution.py:16
  46.2 2.9 %gather_fusion = bf16[21,128,128]{2,1,0:T(8,128)(2,1)} fusion(bf16[45,128,128]{2,1,0:T(8,128)(2,1)} %constant_dynamic-update-slice_fusion, s32[1024]{0:T(1024)S(1)} %pad_clamp_fusion), kind=kCustom, calls=%fused_computation | custom fusion | bytes 1376340 | tf_op jit(solution)/shard_map/jit(_take)/gather | solution.py:51
  49.1 2.4 bitcast_select_fusion
  52.6 4.4 %collective-permute-start.8 = (bf16[640,128]{0,1:T(8,128)(2,1)S(1)}, bf16[640,128]{0,1:T(8,128)(2,1)S(1)}, u32[]{:S(2)}, u32[]{:S(2)}) collective-permute-start(bf16[640,128]{0,1:T(8,128)(2,1)S(1)} %bitcast.58), channel_id=1, source_target_pairs={{0,1},{1,2},{2,3},{3,4},{4,5},{5,6},{6,7},{7,8},{8,9},{9,10},{10,1... | collective-permute-start | bytes 491528 | tf_op jit(solution)/shard_map/ppermute | solution.py:24
  57.0 2.9 %collective-permute-start.9 = (bf16[640,128]{0,1:T(8,128)(2,1)S(1)}, bf16[640,128]{0,1:T(8,128)(2,1)S(1)}, u32[]{:S(2)}, u32[]{:S(2)}) collective-permute-start(bf16[640,128]{0,1:T(8,128)(2,1)S(1)} %bitcast.59), channel_id=1, source_target_pairs={{1,0},{2,1},{3,2},{4,3},{5,4},{6,5},{7,6},{8,7},{9,8},{10,9},{11,1... | collective-permute-start | bytes 491528 | tf_op jit(solution)/shard_map/ppermute | solution.py:27
  61.0 2.3 collective-permute-done.9
  64.0 2.3 multiply_convert_fusion.1
  68.3 135.7 %all-reduce.3.cloned.1.call-done = bf16[640,1920]{1,0:T(8,128)(2,1)} async-done(((bf16[640,1920]{1,0:T(8,128)(2,1)}), bf16[640,1920]{1,0:T(8,128)(2,1)}) %all-reduce.3.cloned.1.call-update) | async-done | bytes 2457616 | tf_op jit(solution)/shard_map/psum | solution.py:60
  204.1 6.0 %fusion = bf16[2688,128]{0,1:T(8,128)(2,1)} fusion(bf16[640,2688]{1,0:T(8,128)(2,1)S(1)} %copy-done, bf16[640,1920]{1,0:T(8,128)(2,1)} %all-reduce.3.cloned.1.call-done, f32[1920]{0:T(1024)S(1)} %get-tuple-element.10, f32[640]{0:T(1024)S(1)} %get-tuple-element.7, f32[1920]{0:T(1024)S(1)} %get-tuple-element.9, f32[640]{0:T(1024)S(1)} %get-tuple-element.6, ...), kind=kOutput, calls=%fused_computation.4 | convolution fusion | flops 772128768 | bytes 7111168 | tf_op jit(solution)/shard_map/dot_general | solution.py:76
  210.1 2.2 copy.15
  214.1 4.5 %collective-permute-start.10 = (bf16[5,128,128]{2,0,1:T(8,128)(2,1)S(1)}, bf16[5,128,128]{2,0,1:T(8,128)(2,1)}, u32[]{:S(2)}, u32[]{:S(2)}) collective-permute-start(bf16[5,128,128]{2,0,1:T(8,128)(2,1)S(1)} %fusion.20), channel_id=1, source_target_pairs={{4,0},{5,1},{6,2},{7,3},{8,4},{9,5},{10,6},{11,7},{12,8},{13,9},{1... | collective-permute-start | bytes 491528 | tf_op jit(solution)/shard_map/ppermute | solution.py:16
  220.3 2.2 collective-permute-start.11
  224.2 2.8 collective-permute-start.12
  228.4 5.4 %collective-permute-start.13 = (bf16[5,128,128]{2,0,1:T(8,128)(2,1)}, bf16[5,128,128]{2,0,1:T(8,128)(2,1)}, u32[]{:S(2)}, u32[]{:S(2)}) collective-permute-start(bf16[5,128,128]{2,0,1:T(8,128)(2,1)} %fusion.29), channel_id=1, source_target_pairs={{1,0},{2,1},{3,2},{4,3},{5,4},{6,5},{7,6},{8,7},{9,8},{10,9},{11,1... | collective-permute-start | bytes 491528 | tf_op jit(solution)/shard_map/ppermute | solution.py:16
  235.1 2.1 collective-permute-start.14
  241.2 5.5 %collective-permute-start.15 = (bf16[5,128,128]{2,0,1:T(8,128)(2,1)}, bf16[5,128,128]{2,0,1:T(8,128)(2,1)}, u32[]{:S(2)}, u32[]{:S(2)}) collective-permute-start(bf16[5,128,128]{2,0,1:T(8,128)(2,1)} %fusion.35), channel_id=1, source_target_pairs={{0,2},{1,3},{2,4},{3,5},{4,6},{5,7},{6,8},{7,9},{8,10},{9,11},{10,... | collective-permute-start | bytes 491528 | tf_op jit(solution)/shard_map/ppermute | solution.py:16
  246.7 5.0 %collective-permute-start.16 = (bf16[5,128,128]{2,0,1:T(8,128)(2,1)}, bf16[5,128,128]{2,0,1:T(8,128)(2,1)}, u32[]{:S(2)}, u32[]{:S(2)}) collective-permute-start(bf16[5,128,128]{2,0,1:T(8,128)(2,1)} %fusion.38), channel_id=1, source_target_pairs={{0,3},{1,4},{2,5},{3,6},{4,7},{5,8},{6,9},{7,10},{8,11},{9,12},{10... | collective-permute-start | bytes 491528 | tf_op jit(solution)/shard_map/ppermute | solution.py:16
  253.6 7.6 %collective-permute-done.16 = bf16[5,128,128]{2,0,1:T(8,128)(2,1)} collective-permute-done((bf16[5,128,128]{2,0,1:T(8,128)(2,1)}, bf16[5,128,128]{2,0,1:T(8,128)(2,1)}, u32[]{:S(2)}, u32[]{:S(2)}) %collective-permute-start.16) | collective-permute-done | bytes 163872 | tf_op jit(solution)/shard_map/ppermute | solution.py:16
  261.2 6.1 %collective-permute-done.17 = bf16[5,128,128]{2,0,1:T(8,128)(2,1)} collective-permute-done((bf16[5,128,128]{2,0,1:T(8,128)(2,1)}, bf16[5,128,128]{2,0,1:T(8,128)(2,1)}, u32[]{:S(2)}, u32[]{:S(2)}) %collective-permute-start.17) | collective-permute-done | bytes 163872 | tf_op jit(solution)/shard_map/ppermute | solution.py:16
  267.4 2.5 convert_add_fusion
  (69 shorter events, 38.3 us)
Async XLA Ops:
  6.5 44.9 %copy-start = (bf16[640,2688]{1,0:T(8,128)(2,1)S(1)}, bf16[640,2688]{1,0:T(8,128)(2,1)}, u32[]{:S(2)}) copy-start(bf16[640,2688]{1,0:T(8,128)(2,1)} %param.5) | copy-start | bytes 10321924
  6.5 197.6 %all-reduce.3.cloned.1.call-start = ((), (), s32[]{:S(2)}) async-start(), calls=%async_computation | async-start | bytes 4915200 | tf_op jit(solution)/shard_map/psum | solution.py:60
  6.5 18.7 %collective-permute-start = (bf16[5,128,128]{2,1,0:T(8,128)(2,1)}, bf16[5,128,128]{2,1,0:T(8,128)(2,1)}, u32[]{:S(2)}, u32[]{:S(2)}) collective-permute-start(bf16[5,128,128]{2,1,0:T(8,128)(2,1)} %bitcast.62), channel_id=1, source_target_pairs={{0,4},{1,5},{2,6},{3,7},{4,8},{5,9},{6,10},{7,11},{8,12},{9,13},{1... | collective-permute-start | bytes 491528 | tf_op jit(solution)/shard_map/ppermute | solution.py:16
  9.7 21.6 %collective-permute-start.1 = (bf16[5,128,128]{2,1,0:T(8,128)(2,1)}, bf16[5,128,128]{2,1,0:T(8,128)(2,1)}, u32[]{:S(2)}, u32[]{:S(2)}) collective-permute-start(bf16[5,128,128]{2,1,0:T(8,128)(2,1)} %bitcast.63), channel_id=1, source_target_pairs={{0,3},{1,4},{2,5},{3,6},{4,7},{5,8},{6,9},{7,10},{8,11},{9,12},{10... | collective-permute-start | bytes 491528 | tf_op jit(solution)/shard_map/ppermute | solution.py:16
  11.8 23.1 %collective-permute-start.2 = (bf16[5,128,128]{2,1,0:T(8,128)(2,1)}, bf16[5,128,128]{2,1,0:T(8,128)(2,1)}, u32[]{:S(2)}, u32[]{:S(2)}) collective-permute-start(bf16[5,128,128]{2,1,0:T(8,128)(2,1)} %bitcast.64), channel_id=1, source_target_pairs={{0,2},{1,3},{2,4},{3,5},{4,6},{5,7},{6,8},{7,9},{8,10},{9,11},{10,... | collective-permute-start | bytes 491528 | tf_op jit(solution)/shard_map/ppermute | solution.py:16
  16.7 22.6 %collective-permute-start.3 = (bf16[5,128,128]{2,1,0:T(8,128)(2,1)}, bf16[5,128,128]{2,1,0:T(8,128)(2,1)}, u32[]{:S(2)}, u32[]{:S(2)}) collective-permute-start(bf16[5,128,128]{2,1,0:T(8,128)(2,1)} %bitcast.65), channel_id=1, source_target_pairs={{0,1},{1,2},{2,3},{3,4},{4,5},{5,6},{6,7},{7,8},{8,9},{9,10},{10,1... | collective-permute-start | bytes 491528 | tf_op jit(solution)/shard_map/ppermute | solution.py:16
  18.6 23.9 %collective-permute-start.4 = (bf16[5,128,128]{2,1,0:T(8,128)(2,1)}, bf16[5,128,128]{2,1,0:T(8,128)(2,1)}, u32[]{:S(2)}, u32[]{:S(2)}) collective-permute-start(bf16[5,128,128]{2,1,0:T(8,128)(2,1)} %bitcast.66), channel_id=1, source_target_pairs={{1,0},{2,1},{3,2},{4,3},{5,4},{6,5},{7,6},{8,7},{9,8},{10,9},{11,1... | collective-permute-start | bytes 491528 | tf_op jit(solution)/shard_map/ppermute | solution.py:16
  25.2 18.9 %collective-permute-start.5 = (bf16[5,128,128]{2,1,0:T(8,128)(2,1)}, bf16[5,128,128]{2,1,0:T(8,128)(2,1)S(1)}, u32[]{:S(2)}, u32[]{:S(2)}) collective-permute-start(bf16[5,128,128]{2,1,0:T(8,128)(2,1)} %bitcast.67), channel_id=1, source_target_pairs={{2,0},{3,1},{4,2},{5,3},{6,4},{7,5},{8,6},{9,7},{10,8},{11,9},{12,... | collective-permute-start | bytes 491528 | tf_op jit(solution)/shard_map/ppermute | solution.py:16
  31.3 13.5 %collective-permute-start.6 = (bf16[5,128,128]{2,1,0:T(8,128)(2,1)}, bf16[5,128,128]{2,1,0:T(8,128)(2,1)S(1)}, u32[]{:S(2)}, u32[]{:S(2)}) collective-permute-start(bf16[5,128,128]{2,1,0:T(8,128)(2,1)} %bitcast.68), channel_id=1, source_target_pairs={{3,0},{4,1},{5,2},{6,3},{7,4},{8,5},{9,6},{10,7},{11,8},{12,9},{13... | collective-permute-start | bytes 491528 | tf_op jit(solution)/shard_map/ppermute | solution.py:16
  34.8 10.6 %collective-permute-start.7 = (bf16[5,128,128]{2,1,0:T(8,128)(2,1)}, bf16[5,128,128]{2,1,0:T(8,128)(2,1)S(1)}, u32[]{:S(2)}, u32[]{:S(2)}) collective-permute-start(bf16[5,128,128]{2,1,0:T(8,128)(2,1)} %bitcast.69), channel_id=1, source_target_pairs={{4,0},{5,1},{6,2},{7,3},{8,4},{9,5},{10,6},{11,7},{12,8},{13,9},{1... | collective-permute-start | bytes 491528 | tf_op jit(solution)/shard_map/ppermute | solution.py:16
  52.6 10.7 %copy-start.2 = (bf16[128,640]{1,0:T(8,128)(2,1)}, bf16[128,640]{1,0:T(8,128)(2,1)S(1)}, u32[]{:S(2)}) copy-start(bf16[128,640]{1,0:T(8,128)(2,1)S(1)} %convolution_convert_fusion) | copy-start | bytes 491524
  52.6 151.5 %copy-start.6 = (f32[640]{0:T(1024)S(1)}, f32[640]{0:T(1024)}, u32[]{:S(2)}) copy-start(f32[640]{0:T(1024)} %param.9) | copy-start | bytes 7684
  52.6 8.4 %collective-permute-start.8 = (bf16[640,128]{0,1:T(8,128)(2,1)S(1)}, bf16[640,128]{0,1:T(8,128)(2,1)S(1)}, u32[]{:S(2)}, u32[]{:S(2)}) collective-permute-start(bf16[640,128]{0,1:T(8,128)(2,1)S(1)} %bitcast.58), channel_id=1, source_target_pairs={{0,1},{1,2},{2,3},{3,4},{4,5},{5,6},{6,7},{7,8},{8,9},{9,10},{10,1... | collective-permute-start | bytes 491528 | tf_op jit(solution)/shard_map/ppermute | solution.py:24
  57.0 6.3 %collective-permute-start.9 = (bf16[640,128]{0,1:T(8,128)(2,1)S(1)}, bf16[640,128]{0,1:T(8,128)(2,1)S(1)}, u32[]{:S(2)}, u32[]{:S(2)}) collective-permute-start(bf16[640,128]{0,1:T(8,128)(2,1)S(1)} %bitcast.59), channel_id=1, source_target_pairs={{1,0},{2,1},{3,2},{4,3},{5,4},{6,5},{7,6},{8,7},{9,8},{10,9},{11,1... | collective-permute-start | bytes 491528 | tf_op jit(solution)/shard_map/ppermute | solution.py:27
  204.1 8.2 %copy-start.5 = (s32[1,21]{1,0:T(1,128)S(1)}, s32[1,21]{1,0:T(1,128)}, u32[]{:S(2)}) copy-start(s32[1,21]{1,0:T(1,128)} %param.7) | copy-start | bytes 256
  212.3 14.7 %copy-start.1 = (bf16[2688,128]{1,0:T(8,128)(2,1)S(1)}, bf16[2688,128]{1,0:T(8,128)(2,1)}, u32[]{:S(2)}) copy-start(bf16[2688,128]{1,0:T(8,128)(2,1)} %copy.15) | copy-start | bytes 2064388
  214.1 27.1 %collective-permute-start.10 = (bf16[5,128,128]{2,0,1:T(8,128)(2,1)S(1)}, bf16[5,128,128]{2,0,1:T(8,128)(2,1)}, u32[]{:S(2)}, u32[]{:S(2)}) collective-permute-start(bf16[5,128,128]{2,0,1:T(8,128)(2,1)S(1)} %fusion.20), channel_id=1, source_target_pairs={{4,0},{5,1},{6,2},{7,3},{8,4},{9,5},{10,6},{11,7},{12,8},{13,9},{1... | collective-permute-start | bytes 491528 | tf_op jit(solution)/shard_map/ppermute | solution.py:16
  220.3 26.4 %collective-permute-start.11 = (bf16[5,128,128]{2,0,1:T(8,128)(2,1)S(1)}, bf16[5,128,128]{2,0,1:T(8,128)(2,1)}, u32[]{:S(2)}, u32[]{:S(2)}) collective-permute-start(bf16[5,128,128]{2,0,1:T(8,128)(2,1)S(1)} %fusion.23), channel_id=1, source_target_pairs={{3,0},{4,1},{5,2},{6,3},{7,4},{8,5},{9,6},{10,7},{11,8},{12,9},{13... | collective-permute-start | bytes 491528 | tf_op jit(solution)/shard_map/ppermute | solution.py:16
  224.2 27.4 %collective-permute-start.12 = (bf16[5,128,128]{2,0,1:T(8,128)(2,1)S(1)}, bf16[5,128,128]{2,0,1:T(8,128)(2,1)}, u32[]{:S(2)}, u32[]{:S(2)}) collective-permute-start(bf16[5,128,128]{2,0,1:T(8,128)(2,1)S(1)} %fusion.26), channel_id=1, source_target_pairs={{2,0},{3,1},{4,2},{5,3},{6,4},{7,5},{8,6},{9,7},{10,8},{11,9},{12,... | collective-permute-start | bytes 491528 | tf_op jit(solution)/shard_map/ppermute | solution.py:16
  228.4 25.2 %collective-permute-start.13 = (bf16[5,128,128]{2,0,1:T(8,128)(2,1)}, bf16[5,128,128]{2,0,1:T(8,128)(2,1)}, u32[]{:S(2)}, u32[]{:S(2)}) collective-permute-start(bf16[5,128,128]{2,0,1:T(8,128)(2,1)} %fusion.29), channel_id=1, source_target_pairs={{1,0},{2,1},{3,2},{4,3},{5,4},{6,5},{7,6},{8,7},{9,8},{10,9},{11,1... | collective-permute-start | bytes 491528 | tf_op jit(solution)/shard_map/ppermute | solution.py:16
  235.1 18.5 %collective-permute-start.14 = (bf16[5,128,128]{2,0,1:T(8,128)(2,1)}, bf16[5,128,128]{2,0,1:T(8,128)(2,1)}, u32[]{:S(2)}, u32[]{:S(2)}) collective-permute-start(bf16[5,128,128]{2,0,1:T(8,128)(2,1)} %fusion.32), channel_id=1, source_target_pairs={{0,1},{1,2},{2,3},{3,4},{4,5},{5,6},{6,7},{7,8},{8,9},{9,10},{10,1... | collective-permute-start | bytes 491528 | tf_op jit(solution)/shard_map/ppermute | solution.py:16
  241.2 12.4 %collective-permute-start.15 = (bf16[5,128,128]{2,0,1:T(8,128)(2,1)}, bf16[5,128,128]{2,0,1:T(8,128)(2,1)}, u32[]{:S(2)}, u32[]{:S(2)}) collective-permute-start(bf16[5,128,128]{2,0,1:T(8,128)(2,1)} %fusion.35), channel_id=1, source_target_pairs={{0,2},{1,3},{2,4},{3,5},{4,6},{5,7},{6,8},{7,9},{8,10},{9,11},{10,... | collective-permute-start | bytes 491528 | tf_op jit(solution)/shard_map/ppermute | solution.py:16
  246.7 14.5 %collective-permute-start.16 = (bf16[5,128,128]{2,0,1:T(8,128)(2,1)}, bf16[5,128,128]{2,0,1:T(8,128)(2,1)}, u32[]{:S(2)}, u32[]{:S(2)}) collective-permute-start(bf16[5,128,128]{2,0,1:T(8,128)(2,1)} %fusion.38), channel_id=1, source_target_pairs={{0,3},{1,4},{2,5},{3,6},{4,7},{5,8},{6,9},{7,10},{8,11},{9,12},{10... | collective-permute-start | bytes 491528 | tf_op jit(solution)/shard_map/ppermute | solution.py:16
  251.7 15.7 %collective-permute-start.17 = (bf16[5,128,128]{2,0,1:T(8,128)(2,1)}, bf16[5,128,128]{2,0,1:T(8,128)(2,1)}, u32[]{:S(2)}, u32[]{:S(2)}) collective-permute-start(bf16[5,128,128]{2,0,1:T(8,128)(2,1)} %fusion.41), channel_id=1, source_target_pairs={{0,4},{1,5},{2,6},{3,7},{4,8},{5,9},{6,10},{7,11},{8,12},{9,13},{1... | collective-permute-start | bytes 491528 | tf_op jit(solution)/shard_map/ppermute | solution.py:16
  (2 other events, 3.0 us)
Sparse Core Ops, SparseCore 0:
  66.4 137.6 all-reduce.2
where the time goes:
time: 279 us; the launch traced here: 277 us
  waiting for transfers between devices  153 us (55%)
  starting transfers between devices  63.2 us (23%)
  matrix products  23.8 us (9%)
  local copies, waits for them, and re-layouts  20.1 us (7%)
  between operations  13.8 us (5%)
  other arithmetic  3.73 us (1%)
    psum x1, waiting for transfers between devices, shards(): lax.psum(partial_value.astype(jnp.bfloat16), 'coef').astype(jnp.float32)  136 us
    ppermute x16, starting transfers between devices, from_behind(): return lax.ppermute(block, axis, route)  55.9 us
    dot_general x9, matrix products, shards(): contribs[offset] = jnp.einsum('js,sro->jro', select, tiles)  14.4 us
    ppermute x16, waiting for transfers between devices, from_behind(): return lax.ppermute(block, axis, route)  13.8 us
    unnamed x22, local copies, waits for them, and re-layouts  11.6 us
    dot_general x1, matrix products, shards(): lax.dot_general(basis_values, weighted, (((0,), (0,)), ((), ())), preferr...  5.96 us
  transfers between devices with their start and end apart: 19, of which 5 were waited for; matrix products, arithmetic and copies ran while one was open for 9% of the time, Pallas kernels for 0%

commit v1 on v0

--- a/solution.py
+++ b/solution.py
@@ -57,7 +57,9 @@
         field, near, (((1,), (1,)), ((), ())), preferred_element_type=jnp.float32
     )
     partial_value = partial_value / jnp.sqrt(jnp.float32(ORBITALS))
-    density = lax.psum(partial_value.astype(jnp.bfloat16), "coef").astype(jnp.float32)
+    density = jnp.sum(lax.all_gather(partial_value.astype(jnp.bfloat16), "coef"), axis=0).astype(
+        jnp.float32
+    )
     anchor = jnp.zeros((), jnp.int32)
     start = batch * points
     padded_centres = jnp.pad(centres, ((0, 0), (points, points)))

time: 279 us -> 545 us (1.95)
  the two profiles are of different devices: /device:TPU:388 before, /device:TPU:390 now
where the time goes in v1:
time: 545 us; the launch traced here: 544 us
  waiting for transfers between devices  406 us (74%)
  starting transfers between devices  64 us (12%)
  matrix products  23.8 us (4%)
  local copies, waits for them, and re-layouts  20.1 us (4%)
  other arithmetic  16.1 us (3%)
  between operations  13.7 us (3%)
    all_gather x1, waiting for transfers between devices, shards(): lax.all_gather(partial_value.astype(jnp.bfloat16), 'coef')  389 us
    ppermute x16, starting transfers between devices, from_behind(): return lax.ppermute(block, axis, route)  56.8 us
    dot_general x9, matrix products, shards(): contribs[offset] = jnp.einsum('js,sro->jro', select, tiles)  14.4 us
    ppermute x16, waiting for transfers between devices, from_behind(): return lax.ppermute(block, axis, route)  13.8 us
    reduce_sum x1, other arithmetic, shards(): jnp.sum(lax.all_gather(partial_value.astype(jnp.bfloat16), 'coef'), axis=0)  12.4 us
    unnamed x22, local copies, waits for them, and re-layouts  11.6 us
  transfers between devices with their start and end apart: 19, of which 5 were waited for; matrix products, arithmetic and copies ran while one was open for 4% of the time, Pallas kernels for 0%

profile of v1, /device:TPU:390, one launch (start us, length us, event | category | flops | bytes accessed | tf_op | source)
XLA Modules:
  0.0 543.8 jit_solution(5728147668214267611)
XLA Ops:
  6.5 3.2 collective-permute-start
  9.7 2.9 collective-permute-start.1
  12.7 4.0 collective-permute-start.2
  18.6 5.1 collective-permute-start.4
  25.2 5.4 collective-permute-start.5
  35.7 2.9 collective-permute-start.7
  47.1 2.9 gather_fusion
  50.0 2.4 bitcast_select_fusion
  53.5 3.4 collective-permute-start.8
  56.9 3.8 collective-permute-start.9
  64.2 2.3 multiply_convert_fusion.1
  68.6 389.4 %all-gather.3.cloned.1.call-done = bf16[5120,1920]{1,0:T(8,128)(2,1)} async-done(((bf16[640,1920]{1,0:T(8,128)(2,1)}), bf16[5120,1920]{1,0:T(8,128)(2,1)}) %all-gather.3.cloned.1.call-update) | async-done | bytes 19660816 | tf_op jit(solution)/shard_map/all_gather | solution.py:60
  458.0 12.4 %reduce_sum.12 = bf16[640,1920]{1,0:T(8,128)(2,1)} reduce(bf16[8,640,1920]{2,1,0:T(8,128)(2,1)} %bitcast.59, bf16[]{:T(256)} %constant.22.clone.1), dimensions={0}, to_apply=%region_0.1 | reduce | flops 8601600 | bytes 22118402 | tf_op jit(solution)/shard_map/reduce_sum | solution.py:60
  470.3 6.0 %fusion = bf16[2688,128]{0,1:T(8,128)(2,1)} fusion(bf16[640,2688]{1,0:T(8,128)(2,1)S(1)} %copy-done, bf16[640,1920]{1,0:T(8,128)(2,1)} %reduce_sum.12, f32[1920]{0:T(1024)S(1)} %get-tuple-element.10, f32[640]{0:T(1024)S(1)} %get-tuple-element.7, f32[1920]{0:T(1024)S(1)} %get-tuple-element.9, f32[640]{0:T(1024)S(1)} %get-tuple-element.6, ...), kind=kOutput, calls=%fused_computation.4 | convolution fusion | flops 772128768 | bytes 7111168 | tf_op jit(solution)/shard_map/dot_general | solution.py:78
  476.3 2.2 copy.15
  480.3 4.5 collective-permute-start.10
  486.6 2.4 collective-permute-start.11
  490.7 3.1 collective-permute-start.12
  495.2 5.1 collective-permute-start.13
  507.8 5.2 collective-permute-start.15
  512.9 5.0 collective-permute-start.16
  519.9 7.7 %collective-permute-done.16 = bf16[5,128,128]{2,0,1:T(8,128)(2,1)} collective-permute-done((bf16[5,128,128]{2,0,1:T(8,128)(2,1)}, bf16[5,128,128]{2,0,1:T(8,128)(2,1)}, u32[]{:S(2)}, u32[]{:S(2)}) %collective-permute-start.16) | collective-permute-done | bytes 163872 | tf_op jit(solution)/shard_map/ppermute | solution.py:16
  527.6 6.1 %collective-permute-done.17 = bf16[5,128,128]{2,0,1:T(8,128)(2,1)} collective-permute-done((bf16[5,128,128]{2,0,1:T(8,128)(2,1)}, bf16[5,128,128]{2,0,1:T(8,128)(2,1)}, u32[]{:S(2)}, u32[]{:S(2)}) %collective-permute-start.17) | collective-permute-done | bytes 163872 | tf_op jit(solution)/shard_map/ppermute | solution.py:16
  533.7 2.5 convert_add_fusion
  (70 shorter events, 40.1 us)
Async XLA Ops:
  6.5 45.8 %copy-start = (bf16[640,2688]{1,0:T(8,128)(2,1)S(1)}, bf16[640,2688]{1,0:T(8,128)(2,1)}, u32[]{:S(2)}) copy-start(bf16[640,2688]{1,0:T(8,128)(2,1)} %param.5) | copy-start | bytes 10321924
  6.5 451.4 %all-gather.3.cloned.1.call-start = ((), (), s32[]{:S(2)}) async-start(), calls=%async_computation | async-start | bytes 22118400 | tf_op jit(solution)/shard_map/all_gather | solution.py:60
  6.5 18.7 %collective-permute-start = (bf16[5,128,128]{2,1,0:T(8,128)(2,1)}, bf16[5,128,128]{2,1,0:T(8,128)(2,1)}, u32[]{:S(2)}, u32[]{:S(2)}) collective-permute-start(bf16[5,128,128]{2,1,0:T(8,128)(2,1)} %bitcast.64), channel_id=1, source_target_pairs={{0,4},{1,5},{2,6},{3,7},{4,8},{5,9},{6,10},{7,11},{8,12},{9,13},{1... | collective-permute-start | bytes 491528 | tf_op jit(solution)/shard_map/ppermute | solution.py:16
  9.7 22.5 %collective-permute-start.1 = (bf16[5,128,128]{2,1,0:T(8,128)(2,1)}, bf16[5,128,128]{2,1,0:T(8,128)(2,1)}, u32[]{:S(2)}, u32[]{:S(2)}) collective-permute-start(bf16[5,128,128]{2,1,0:T(8,128)(2,1)} %bitcast.65), channel_id=1, source_target_pairs={{0,3},{1,4},{2,5},{3,6},{4,7},{5,8},{6,9},{7,10},{8,11},{9,12},{10... | collective-permute-start | bytes 491528 | tf_op jit(solution)/shard_map/ppermute | solution.py:16
  12.7 23.1 %collective-permute-start.2 = (bf16[5,128,128]{2,1,0:T(8,128)(2,1)}, bf16[5,128,128]{2,1,0:T(8,128)(2,1)}, u32[]{:S(2)}, u32[]{:S(2)}) collective-permute-start(bf16[5,128,128]{2,1,0:T(8,128)(2,1)} %bitcast.66), channel_id=1, source_target_pairs={{0,2},{1,3},{2,4},{3,5},{4,6},{5,7},{6,8},{7,9},{8,10},{9,11},{10,... | collective-permute-start | bytes 491528 | tf_op jit(solution)/shard_map/ppermute | solution.py:16
  16.7 23.5 %collective-permute-start.3 = (bf16[5,128,128]{2,1,0:T(8,128)(2,1)}, bf16[5,128,128]{2,1,0:T(8,128)(2,1)}, u32[]{:S(2)}, u32[]{:S(2)}) collective-permute-start(bf16[5,128,128]{2,1,0:T(8,128)(2,1)} %bitcast.67), channel_id=1, source_target_pairs={{0,1},{1,2},{2,3},{3,4},{4,5},{5,6},{6,7},{7,8},{8,9},{9,10},{10,1... | collective-permute-start | bytes 491528 | tf_op jit(solution)/shard_map/ppermute | solution.py:16
  18.6 24.8 %collective-permute-start.4 = (bf16[5,128,128]{2,1,0:T(8,128)(2,1)}, bf16[5,128,128]{2,1,0:T(8,128)(2,1)}, u32[]{:S(2)}, u32[]{:S(2)}) collective-permute-start(bf16[5,128,128]{2,1,0:T(8,128)(2,1)} %bitcast.68), channel_id=1, source_target_pairs={{1,0},{2,1},{3,2},{4,3},{5,4},{6,5},{7,6},{8,7},{9,8},{10,9},{11,1... | collective-permute-start | bytes 491528 | tf_op jit(solution)/shard_map/ppermute | solution.py:16
  25.2 19.8 %collective-permute-start.5 = (bf16[5,128,128]{2,1,0:T(8,128)(2,1)}, bf16[5,128,128]{2,1,0:T(8,128)(2,1)S(1)}, u32[]{:S(2)}, u32[]{:S(2)}) collective-permute-start(bf16[5,128,128]{2,1,0:T(8,128)(2,1)} %bitcast.69), channel_id=1, source_target_pairs={{2,0},{3,1},{4,2},{5,3},{6,4},{7,5},{8,6},{9,7},{10,8},{11,9},{12,... | collective-permute-start | bytes 491528 | tf_op jit(solution)/shard_map/ppermute | solution.py:16
  32.2 13.5 %collective-permute-start.6 = (bf16[5,128,128]{2,1,0:T(8,128)(2,1)}, bf16[5,128,128]{2,1,0:T(8,128)(2,1)S(1)}, u32[]{:S(2)}, u32[]{:S(2)}) collective-permute-start(bf16[5,128,128]{2,1,0:T(8,128)(2,1)} %bitcast.70), channel_id=1, source_target_pairs={{3,0},{4,1},{5,2},{6,3},{7,4},{8,5},{9,6},{10,7},{11,8},{12,9},{13... | collective-permute-start | bytes 491528 | tf_op jit(solution)/shard_map/ppermute | solution.py:16
  35.7 10.6 %collective-permute-start.7 = (bf16[5,128,128]{2,1,0:T(8,128)(2,1)}, bf16[5,128,128]{2,1,0:T(8,128)(2,1)S(1)}, u32[]{:S(2)}, u32[]{:S(2)}) collective-permute-start(bf16[5,128,128]{2,1,0:T(8,128)(2,1)} %bitcast.71), channel_id=1, source_target_pairs={{4,0},{5,1},{6,2},{7,3},{8,4},{9,5},{10,6},{11,7},{12,8},{13,9},{1... | collective-permute-start | bytes 491528 | tf_op jit(solution)/shard_map/ppermute | solution.py:16
  53.5 10.1 %copy-start.2 = (bf16[128,640]{1,0:T(8,128)(2,1)}, bf16[128,640]{1,0:T(8,128)(2,1)S(1)}, u32[]{:S(2)}) copy-start(bf16[128,640]{1,0:T(8,128)(2,1)S(1)} %convolution_convert_fusion) | copy-start | bytes 491524
  53.5 8.3 %collective-permute-start.8 = (bf16[640,128]{0,1:T(8,128)(2,1)S(1)}, bf16[640,128]{0,1:T(8,128)(2,1)S(1)}, u32[]{:S(2)}, u32[]{:S(2)}) collective-permute-start(bf16[640,128]{0,1:T(8,128)(2,1)S(1)} %bitcast.60), channel_id=1, source_target_pairs={{0,1},{1,2},{2,3},{3,4},{4,5},{5,6},{6,7},{7,8},{8,9},{9,10},{10,1... | collective-permute-start | bytes 491528 | tf_op jit(solution)/shard_map/ppermute | solution.py:24
  56.9 6.7 %collective-permute-start.9 = (bf16[640,128]{0,1:T(8,128)(2,1)S(1)}, bf16[640,128]{0,1:T(8,128)(2,1)S(1)}, u32[]{:S(2)}, u32[]{:S(2)}) collective-permute-start(bf16[640,128]{0,1:T(8,128)(2,1)S(1)} %bitcast.61), channel_id=1, source_target_pairs={{1,0},{2,1},{3,2},{4,3},{5,4},{6,5},{7,6},{8,7},{9,8},{10,9},{11,1... | collective-permute-start | bytes 491528 | tf_op jit(solution)/shard_map/ppermute | solution.py:27
  458.0 12.4 %copy-start.6 = (f32[640]{0:T(1024)S(1)}, f32[640]{0:T(1024)}, u32[]{:S(2)}) copy-start(f32[640]{0:T(1024)} %param.9) | copy-start | bytes 7684
  470.3 8.2 %copy-start.5 = (s32[1,21]{1,0:T(1,128)S(1)}, s32[1,21]{1,0:T(1,128)}, u32[]{:S(2)}) copy-start(s32[1,21]{1,0:T(1,128)} %param.7) | copy-start | bytes 256
  478.5 15.3 %copy-start.1 = (bf16[2688,128]{1,0:T(8,128)(2,1)S(1)}, bf16[2688,128]{1,0:T(8,128)(2,1)}, u32[]{:S(2)}) copy-start(bf16[2688,128]{1,0:T(8,128)(2,1)} %copy.15) | copy-start | bytes 2064388
  480.3 27.4 %collective-permute-start.10 = (bf16[5,128,128]{2,0,1:T(8,128)(2,1)S(1)}, bf16[5,128,128]{2,0,1:T(8,128)(2,1)}, u32[]{:S(2)}, u32[]{:S(2)}) collective-permute-start(bf16[5,128,128]{2,0,1:T(8,128)(2,1)S(1)} %fusion.20), channel_id=1, source_target_pairs={{4,0},{5,1},{6,2},{7,3},{8,4},{9,5},{10,6},{11,7},{12,8},{13,9},{1... | collective-permute-start | bytes 491528 | tf_op jit(solution)/shard_map/ppermute | solution.py:16
  486.6 26.4 %collective-permute-start.11 = (bf16[5,128,128]{2,0,1:T(8,128)(2,1)S(1)}, bf16[5,128,128]{2,0,1:T(8,128)(2,1)}, u32[]{:S(2)}, u32[]{:S(2)}) collective-permute-start(bf16[5,128,128]{2,0,1:T(8,128)(2,1)S(1)} %fusion.23), channel_id=1, source_target_pairs={{3,0},{4,1},{5,2},{6,3},{7,4},{8,5},{9,6},{10,7},{11,8},{12,9},{13... | collective-permute-start | bytes 491528 | tf_op jit(solution)/shard_map/ppermute | solution.py:16
  490.7 27.2 %collective-permute-start.12 = (bf16[5,128,128]{2,0,1:T(8,128)(2,1)S(1)}, bf16[5,128,128]{2,0,1:T(8,128)(2,1)}, u32[]{:S(2)}, u32[]{:S(2)}) collective-permute-start(bf16[5,128,128]{2,0,1:T(8,128)(2,1)S(1)} %fusion.26), channel_id=1, source_target_pairs={{2,0},{3,1},{4,2},{5,3},{6,4},{7,5},{8,6},{9,7},{10,8},{11,9},{12,... | collective-permute-start | bytes 491528 | tf_op jit(solution)/shard_map/ppermute | solution.py:16
  495.2 24.7 %collective-permute-start.13 = (bf16[5,128,128]{2,0,1:T(8,128)(2,1)}, bf16[5,128,128]{2,0,1:T(8,128)(2,1)}, u32[]{:S(2)}, u32[]{:S(2)}) collective-permute-start(bf16[5,128,128]{2,0,1:T(8,128)(2,1)} %fusion.29), channel_id=1, source_target_pairs={{1,0},{2,1},{3,2},{4,3},{5,4},{6,5},{7,6},{8,7},{9,8},{10,9},{11,1... | collective-permute-start | bytes 491528 | tf_op jit(solution)/shard_map/ppermute | solution.py:16
  501.6 18.2 %collective-permute-start.14 = (bf16[5,128,128]{2,0,1:T(8,128)(2,1)}, bf16[5,128,128]{2,0,1:T(8,128)(2,1)}, u32[]{:S(2)}, u32[]{:S(2)}) collective-permute-start(bf16[5,128,128]{2,0,1:T(8,128)(2,1)} %fusion.32), channel_id=1, source_target_pairs={{0,1},{1,2},{2,3},{3,4},{4,5},{5,6},{6,7},{7,8},{8,9},{9,10},{10,1... | collective-permute-start | bytes 491528 | tf_op jit(solution)/shard_map/ppermute | solution.py:16
  507.8 12.1 %collective-permute-start.15 = (bf16[5,128,128]{2,0,1:T(8,128)(2,1)}, bf16[5,128,128]{2,0,1:T(8,128)(2,1)}, u32[]{:S(2)}, u32[]{:S(2)}) collective-permute-start(bf16[5,128,128]{2,0,1:T(8,128)(2,1)} %fusion.35), channel_id=1, source_target_pairs={{0,2},{1,3},{2,4},{3,5},{4,6},{5,7},{6,8},{7,9},{8,10},{9,11},{10,... | collective-permute-start | bytes 491528 | tf_op jit(solution)/shard_map/ppermute | solution.py:16
  512.9 14.7 %collective-permute-start.16 = (bf16[5,128,128]{2,0,1:T(8,128)(2,1)}, bf16[5,128,128]{2,0,1:T(8,128)(2,1)}, u32[]{:S(2)}, u32[]{:S(2)}) collective-permute-start(bf16[5,128,128]{2,0,1:T(8,128)(2,1)} %fusion.38), channel_id=1, source_target_pairs={{0,3},{1,4},{2,5},{3,6},{4,7},{5,8},{6,9},{7,10},{8,11},{9,12},{10... | collective-permute-start | bytes 491528 | tf_op jit(solution)/shard_map/ppermute | solution.py:16
  517.9 15.8 %collective-permute-start.17 = (bf16[5,128,128]{2,0,1:T(8,128)(2,1)}, bf16[5,128,128]{2,0,1:T(8,128)(2,1)}, u32[]{:S(2)}, u32[]{:S(2)}) collective-permute-start(bf16[5,128,128]{2,0,1:T(8,128)(2,1)} %fusion.41), channel_id=1, source_target_pairs={{0,4},{1,5},{2,6},{3,7},{4,8},{5,9},{6,10},{7,11},{8,12},{9,13},{1... | collective-permute-start | bytes 491528 | tf_op jit(solution)/shard_map/ppermute | solution.py:16
  (2 other events, 2.4 us)
Sparse Core Ops, SparseCore 0:
  66.7 391.2 all-gather.2
